TPU v7x, 32 devices: a whole 2x2x4 slice. The times are simulated.
32 devices in a mesh: seq: 8 (over z, y), dp: 4 (over x, core).
Axes of the slice: x: 2, y: 2, z: 4, core: 2. Of those that a mesh axis runs over, the one named last changes fastest.
Arguments:
- layer_rows: bfloat16 [4, 1024, 1024], P('dp', 'seq'), may hold values from -6 to 6
- doc_ids: int32 [4, 1024], P('dp', 'seq'), may hold values from 0 to 5, never falling along the last dimension, each value on 1 to 512 neighbouring positions
- packing: int32 [4, 8], P('dp'), may hold values from 0 to 7, each once within a row
- norm_gain: float32 [1024], replicated, may hold values from 0.1 to 1.9
- w_qkv: bfloat16 [1024, 3072], replicated, may hold values from -0.1875 to 0.1875
- d_attn: bfloat16 [4, 1024, 1024], P('dp', 'seq'), may hold values from -6 to 6
Outputs:
- d_input: bfloat16 [4, 1024, 1024], P('dp', 'seq')
- w_grad: float32 [1024, 3072], P('seq')
Inputs may be any that keep to these rules, and one draw needn't show every extreme that they name: `doc_ids`: in each group the song numbers never fall along the initial order; every number occurs, and one song spans exactly 512 frames. `packing`: each group's row names every block number once.
All inputs are finite; a program needn't handle non-finite values.
Results may differ from a plain program's by a relative error of at most 0.024.
Values may be sent and summed in bfloat16 or wider, within the bound.
A program may use at most 128 MiB of HBM per device.

v0:
```python
import math

import jax
import jax.numpy as jnp
from jax import lax
from jax.sharding import PartitionSpec as P

HEADS = 8
HEAD = 128
BLOCK = 128


def rounded(value):
    return lax.optimization_barrier(value.astype(jnp.bfloat16)).astype(jnp.float32)


def normalize(frames, norm_gain):
    values = frames.astype(jnp.float32)
    inverse = lax.rsqrt(jnp.mean(values * values, axis=-1, keepdims=True) + 1e-05)
    unit_rows = values * inverse
    return (inverse, unit_rows, (unit_rows * norm_gain).astype(jnp.bfloat16))


def body(layer_rows, doc_ids, packing, norm_gain, w_qkv, d_attn):
    shards = lax.axis_size("seq")
    my_index = lax.axis_index("seq")
    frames = layer_rows[0]
    tok_rows = frames.shape[0]
    head_cols = HEADS * HEAD
    total_keys = tok_rows * shards
    block_order = packing[0]
    key_pos = (block_order[:, None] * BLOCK + jnp.arange(BLOCK, dtype=jnp.int32)[None, :]).reshape(
        total_keys
    )
    first_own = my_index * tok_rows
    my_pos = lax.dynamic_slice_in_dim(key_pos, first_own, tok_rows, 0)
    doc_low = doc_ids[0].astype(jnp.bfloat16)
    pieces = (
        lax.all_gather(frames, "seq", axis=0, tiled=True),
        lax.all_gather(doc_low, "seq", axis=0, tiled=True),
    )
    length = pieces[0].shape[0]
    inside = (my_pos >= 0) & (my_pos < length)
    clipped = jnp.clip(my_pos, 0, length - 1)
    new_rows = jnp.where(
        inside[:, None], jnp.take(pieces[0], clipped, axis=0), jnp.zeros_like(frames)
    )
    new_docs = jnp.where(inside, jnp.take(pieces[1], clipped, axis=0), jnp.zeros_like(doc_low))
    inverse, unit_rows, normed = normalize(new_rows, norm_gain)
    projected = jnp.dot(normed, w_qkv, preferred_element_type=jnp.float32).astype(jnp.bfloat16)
    queries = projected[:, :head_cols]
    all_keys, all_values, key_docs_low = (
        lax.all_gather(projected[:, head_cols : 2 * head_cols], "seq", axis=0, tiled=True),
        lax.all_gather(projected[:, 2 * head_cols :], "seq", axis=0, tiled=True),
        lax.all_gather(new_docs, "seq", axis=0, tiled=True),
    )
    key_docs = key_docs_low.astype(jnp.int32)
    my_docs = lax.dynamic_slice_in_dim(key_docs, first_own, tok_rows, 0)
    factor = 1.0 / math.sqrt(HEAD)
    q_heads = queries.reshape(tok_rows, HEADS, HEAD)
    grad_heads = d_attn[0].reshape(tok_rows, HEADS, HEAD)
    group_count = total_keys // total_keys

    def key_slab(group_idx):
        first_key = group_idx * total_keys
        slab_keys = all_keys.reshape(total_keys, HEADS, HEAD)
        slab_values = all_values.reshape(total_keys, HEADS, HEAD)
        allowed = (my_docs[:, None] == key_docs[None, :]) & (key_pos[None, :] <= my_pos[:, None])
        return (first_key, slab_keys, slab_values, allowed)

    def exp_scores(query_part, slab_keys, allowed):
        scores = (
            jnp.einsum("qhd,khd->hqk", query_part, slab_keys, preferred_element_type=jnp.float32)
            * factor
        )
        return jnp.where(allowed[None], jnp.exp(scores), jnp.float32(0.0))

    def add_denominator(group_idx, running):
        first_key, slab_keys, slab_values, allowed = key_slab(group_idx)
        return running + jnp.sum(exp_scores(q_heads, slab_keys, allowed), axis=-1)

    denominator = lax.fori_loop(
        0, group_count, add_denominator, jnp.zeros((HEADS, tok_rows), jnp.float32)
    )

    def probabilities(slab_keys, allowed):
        attn_prob = exp_scores(q_heads, slab_keys, allowed) / denominator[:, :, None]
        return (attn_prob, attn_prob.astype(jnp.bfloat16))

    def add_output(group_idx, running):
        first_key, slab_keys, slab_values, allowed = key_slab(group_idx)

        def compute():
            attn_prob, prob_low = probabilities(slab_keys, allowed)
            return jnp.einsum(
                "hqk,khd->qhd", prob_low, slab_values, preferred_element_type=jnp.float32
            )

        return running + compute()

    outputs = lax.fori_loop(
        0, group_count, add_output, jnp.zeros((tok_rows, HEADS, HEAD), jnp.float32)
    )
    row_delta = jnp.sum(grad_heads.astype(jnp.float32) * outputs, axis=-1).T

    def slab_backward(slab_keys, slab_values, allowed):
        attn_prob, prob_low = probabilities(slab_keys, allowed)
        grad_prob = jnp.einsum(
            "qhd,khd->hqk", grad_heads, slab_values, preferred_element_type=jnp.float32
        )
        dscore = (attn_prob * (grad_prob - row_delta[:, :, None])).astype(jnp.bfloat16)
        dq_part = (
            jnp.einsum("hqk,khd->qhd", dscore, slab_keys, preferred_element_type=jnp.float32)
            * factor
        )
        return (dq_part, dscore, prob_low)

    def add_grads(group_idx, running):
        dq_sum, kv_grads = running
        first_key, slab_keys, slab_values, allowed = key_slab(group_idx)

        def compute():
            dq_part, dscore, prob_low = slab_backward(slab_keys, slab_values, allowed)
            dk_part = (
                jnp.einsum("hqk,qhd->khd", dscore, q_heads, preferred_element_type=jnp.float32)
                * factor
            )
            dv_part = jnp.einsum(
                "hqk,qhd->khd", prob_low, grad_heads, preferred_element_type=jnp.float32
            )
            return (
                dq_part,
                jnp.concatenate(
                    [
                        dk_part.reshape(total_keys, head_cols),
                        dv_part.reshape(total_keys, head_cols),
                    ],
                    axis=1,
                ),
            )

        dq_part, kv_part = compute()
        return (dq_sum + dq_part, kv_part)

    dq_sum, kv_grads = lax.fori_loop(
        0,
        group_count,
        add_grads,
        (
            jnp.zeros((tok_rows, HEADS, HEAD), jnp.float32),
            jnp.zeros((total_keys, 2 * head_cols), jnp.float32),
        ),
    )
    summed = lax.psum_scatter(
        rounded(kv_grads).astype(jnp.bfloat16), "seq", scatter_dimension=0, tiled=True
    ).astype(jnp.float32)
    grad_qkv = jnp.concatenate([dq_sum.reshape(tok_rows, head_cols), summed], axis=1).astype(
        jnp.bfloat16
    )
    d_normed = lax.dot_general(
        grad_qkv, w_qkv, (((1,), (1,)), ((), ())), preferred_element_type=jnp.float32
    )
    gained = d_normed * norm_gain
    d_frames = (
        inverse * (gained - unit_rows * jnp.mean(gained * unit_rows, axis=-1, keepdims=True))
    ).astype(jnp.bfloat16)
    w_part = lax.psum_scatter(
        rounded(
            lax.dot_general(
                normed, grad_qkv, (((0,), (0,)), ((), ())), preferred_element_type=jnp.float32
            )
        ).astype(jnp.bfloat16),
        "seq",
        scatter_dimension=0,
        tiled=True,
    )
    w_total = lax.psum(w_part, "dp").astype(jnp.float32)
    w_grad = w_total * (1.0 / math.sqrt(total_keys * lax.axis_size("dp")))
    return (d_frames[None], w_grad)


def solution(mesh):
    return jax.shard_map(
        body,
        mesh=mesh,
        in_specs=(
            P("dp", "seq", None),
            P("dp", "seq"),
            P("dp", None),
            P(),
            P(),
            P("dp", "seq", None),
        ),
        out_specs=(P("dp", "seq", None), P("seq", None)),
        check_vma=False,
    )
```

profile of v0, /device:TPU:0, one launch (start us, length us, event | category | flops | bytes accessed | tf_op | source)
XLA Modules:
  0.0 447.1 jit_solution(5946041160911952398)
XLA Ops:
  7.2 0.0 all-gather.11.cloned.1.call-start
  7.2 0.7 all-gather.11.cloned.1.call-update
  7.9 0.0 all-gather.7.cloned.1.call-start
  7.9 0.7 multiply_bitcast_fusion
  8.6 0.1 add_bitcast_fusion
  8.7 0.1 compare_and_fusion.2
  8.8 53.4 %all-gather.11.cloned.1.call-done = bf16[1,1024,1024]{2,1,0:T(8,128)(2,1)} async-done(((bf16[1,128,1024]{2,1,0:T(8,128)(2,1)}), bf16[1,1024,1024]{2,1,0:T(8,128)(2,1)}) %all-gather.11.cloned.1.call-update) | async-done | bytes 2097168 | tf_op jit(solution)/shard_map/all_gather | solution.py:39
  62.1 2.9 gather_fusion
  65.1 0.2 fusion.16
  65.3 0.0 copy-start.7
  65.3 0.0 copy-start.5
  65.3 3.9 convolution_convert_fusion.1
  69.3 0.8 fusion.24
  70.1 0.0 all-gather.7.cloned.1.call-update
  70.1 0.0 all-gather.9.cloned.1.call-start
  70.2 0.7 all-gather.9.cloned.1.call-update
  70.9 0.0 reduce-scatter.7.cloned.1.call-start
  70.9 0.0 copy-done.7
  70.9 18.0 %all-gather.1 = bf16[1,1024]{1,0:T(2,128)(2,1)S(1)} all-gather(bf16[1,128]{1,0:T(2,128)(2,1)S(1)} %convert_element_type.50), channel_id=3, replica_groups=mesh['seq'=8,'dp'=4] {'seq'}, dimensions={1}, use_global_device_ids=true | all-gather | bytes 2304 | tf_op jit(solution)/shard_map/all_gather | solution.py:40
  88.9 1.3 gather_fusion.1
  90.2 16.5 %all-gather.2 = bf16[8,1,128]{2,1,0:T(2,128)(2,1)S(1)} all-gather(bf16[1,1,128]{2,1,0:T(2,128)(2,1)S(1)} %select_bitcast_fusion), channel_id=1, replica_groups=mesh['seq'=8,'dp'=4] {'seq'}, dimensions={0}, use_global_device_ids=true | all-gather | bytes 2304 | tf_op jit(solution)/shard_map/all_gather | solution.py:55
  106.7 0.1 dynamic_slice.7
  106.8 0.0 copy-done.5
  106.8 0.2 copy.28
  107.0 0.2 compare_and_fusion
  107.2 0.2 copy.40
  107.4 10.7 %all-gather.7.cloned.1.call-done = bf16[1024,1024]{1,0:T(8,128)(2,1)} async-done(((bf16[128,1024]{1,0:T(8,128)(2,1)}), bf16[1024,1024]{1,0:T(8,128)(2,1)}) %all-gather.7.cloned.1.call-update) | async-done | bytes 2097168 | tf_op jit(solution)/shard_map/all_gather | solution.py:53
  118.1 2.9 copy.39
  120.9 1.5 fusion.2
  122.5 0.0 copy-start.1
  122.5 1.9 copy-done.1
  124.4 2.9 convolution_convert_fusion.2
  127.3 41.4 %all-gather.9.cloned.1.call-done = bf16[1024,1024]{1,0:T(8,128)(2,1)} async-done(((bf16[128,1024]{1,0:T(8,128)(2,1)}), bf16[1024,1024]{1,0:T(8,128)(2,1)}) %all-gather.9.cloned.1.call-update) | async-done | bytes 2097168 | tf_op jit(solution)/shard_map/all_gather | solution.py:54
  168.7 3.9 copy.41
  172.6 0.0 copy-start.2
  172.6 0.0 copy-start.3
  172.6 4.3 fusion.5
  176.9 0.0 copy-done.2
  176.9 0.4 copy-done.3
  177.3 1.9 fusion
  179.2 0.0 copy-start
  179.2 1.3 copy-done
  180.6 0.0 copy-start.4
  180.6 0.7 multiply_convert_fusion
  181.3 0.9 copy-done.4
  182.2 2.4 pad_maximum_fusion
  184.6 6.5 %copy.37 = bf16[1024,2048]{1,0:T(8,128)(2,1)} copy(bf16[1024,2048]{0,1:T(8,128)(2,1)} %pad_maximum_fusion) | data formatting | bytes 8388608
  191.1 0.0 copy-start.6
  191.1 0.0 reduce-scatter.7.cloned.1.call-update
  191.2 0.2 reduce-scatter.5.cloned.1.call-start
  191.4 2.3 fusion.4
  193.7 84.2 %reduce-scatter.7.cloned.1.call-done = bf16[128,2048]{1,0:T(8,128)(2,1)} async-done(((bf16[1024,2048]{1,0:T(8,128)(2,1)}), bf16[128,2048]{1,0:T(8,128)(2,1)}) %reduce-scatter.7.cloned.1.call-update) | async-done | bytes 524304
  277.9 1.3 copy.38
  279.2 0.0 copy-done.6
  279.2 4.6 %convolution_convert_fusion = bf16[1024,3072]{1,0:T(8,128)(2,1)} fusion(bf16[128,2048]{0,1:T(8,128)(2,1)S(1)} %copy.38, bf16[128,1024]{0,1:T(8,128)(2,1)S(1)} %bitcast.56, f32[1024]{0:T(1024)S(1)} %copy-done.6, f32[128]{0:T(128)S(1)} %add_rsqrt_fusion, bf16[128,1024]{1,0:T(8,128)(2,1)S(1)} %gather_fusion, pred[128]{0:T(512)(128)(4,1)S(1)} %compare_and_fusion.1, ...), kind=kOutput, calls=%fused_computation.2 | convolution fusion | flops 810811392 | bytes 7344896 | tf_op jit(solution)/shard_map/dot_general | solution.py:169
  283.8 0.0 reduce-scatter.5.cloned.1.call-update
  283.8 0.0 all-reduce.2.cloned.1.call-start
  283.9 5.1 %fusion.12 = (f32[128]{0:T(128)S(1)}, f32[128,1024]{1,0:T(8,128)S(1)}) fusion(f32[128]{0:T(128)S(1)} %add_rsqrt_fusion, bf16[128,1024]{1,0:T(8,128)(2,1)S(1)} %gather_fusion, pred[128]{0:T(512)(128)(4,1)S(1)} %compare_and_fusion.1, pred[128]{0:T(512)(128)(4,1)S(1)} %get-tuple-element.58, f32[1024]{0:T(1024)S(1)} %copy-done.6, ...), kind=kOutput, calls=%fused_computation.28 | convolution fusion | flops 807796608 | bytes 7869696 | tf_op jit(solution)/shard_map/dot_general | solution.py:160
  289.0 112.7 %reduce-scatter.5.cloned.1.call-done = bf16[128,3072]{1,0:T(8,128)(2,1)} async-done(((bf16[1024,3072]{1,0:T(8,128)(2,1)}), bf16[128,3072]{1,0:T(8,128)(2,1)}) %reduce-scatter.5.cloned.1.call-update) | async-done | bytes 786448 | tf_op jit(solution)/shard_map/reduce_scatter | solution.py:167
  401.7 0.0 all-reduce.2.cloned.1.call-update
  401.8 0.9 fusion.17
  402.7 35.2 %all-reduce.2.cloned.1.call-done = bf16[128,3072]{1,0:T(8,128)(2,1)} async-done(((bf16[128,3072]{1,0:T(8,128)(2,1)}), bf16[128,3072]{1,0:T(8,128)(2,1)}) %all-reduce.2.cloned.1.call-update) | async-done | bytes 786448 | tf_op jit(solution)/shard_map/psum | solution.py:177
  437.9 2.4 convert_multiply_fusion
  (9 shorter events, 0.1 us)
Async XLA Ops:
  7.2 55.0 %all-gather.11.cloned.1.call-start = ((), (), s32[]{:S(2)}) async-start(), calls=%async_computation.6 | async-start | bytes 2359296 | tf_op jit(solution)/shard_map/all_gather | solution.py:39
  7.9 110.2 %all-gather.7.cloned.1.call-start = ((), (), s32[]{:S(2)}) async-start(), calls=%async_computation.2 | async-start | bytes 2359296 | tf_op jit(solution)/shard_map/all_gather | solution.py:53
  65.3 5.6 %copy-start.7 = (s32[1,128]{1,0:T(1,128)S(1)}, s32[1,128]{1,0:T(1,128)}, u32[]{:S(2)}) copy-start(s32[1,128]{1,0:T(1,128)} %param.7) | copy-start | bytes 1540
  65.3 41.5 %copy-start.5 = (bf16[1,128,1024]{2,1,0:T(8,128)(2,1)S(1)}, bf16[1,128,1024]{2,1,0:T(8,128)(2,1)}, u32[]{:S(2)}) copy-start(bf16[1,128,1024]{2,1,0:T(8,128)(2,1)} %param.11) | copy-start | bytes 786436
  70.1 98.5 %all-gather.9.cloned.1.call-start = ((), (), s32[]{:S(2)}) async-start(), calls=%async_computation.3 | async-start | bytes 2359296 | tf_op jit(solution)/shard_map/all_gather | solution.py:54
  70.9 207.0 %reduce-scatter.7.cloned.1.call-start = ((), (), s32[]{:S(2)}) async-start(), calls=%async_computation.7 | async-start | bytes 4718592
  122.5 1.9 copy-start.1
  172.6 4.3 copy-start.2
  172.6 4.7 %copy-start.3 = (bf16[1024,1024]{0,1:T(8,128)(2,1)S(1)}, bf16[1024,1024]{0,1:T(8,128)(2,1)}, u32[]{:S(2)}) copy-start(bf16[1024,1024]{0,1:T(8,128)(2,1)} %copy.41) | copy-start | bytes 6291460
  179.2 1.4 copy-start
  180.6 1.6 copy-start.4
  191.1 88.0 %copy-start.6 = (f32[1024]{0:T(1024)S(1)}, f32[1024]{0:T(1024)}, u32[]{:S(2)}) copy-start(f32[1024]{0:T(1024)} %param.9) | copy-start | bytes 12292
  191.2 210.6 %reduce-scatter.5.cloned.1.call-start = ((), (), s32[]{:S(2)}) async-start(), calls=%async_computation.4 | async-start | bytes 7077888 | tf_op jit(solution)/shard_map/reduce_scatter | solution.py:167
  283.8 154.0 %all-reduce.2.cloned.1.call-start = ((), (), s32[]{:S(2)}) async-start(), calls=%async_computation.5 | async-start | bytes 1572864 | tf_op jit(solution)/shard_map/psum | solution.py:177
Sparse Core Ops, SparseCore 0:
  10.1 51.9 all-gather.10
  70.3 47.7 all-gather.6
  120.8 47.8 all-gather.8
  191.3 86.5 reduce-scatter.6
  284.0 117.7 reduce-scatter.4
  404.1 33.7 all-reduce.1
where the time goes:
time: 448 us; the launch traced here: 447 us
  waiting for transfers between devices  339 us (76%)
  blocking collectives  34.5 us (8%)
  matrix products  27.3 us (6%)
  local copies, waits for them, and re-layouts  24.6 us (5%)
  between operations  14.3 us (3%)
  other arithmetic  7.09 us (2%)
    reduce_scatter x1, waiting for transfers between devices, body(): lax.psum_scatter(rounded(lax.dot_general(normed, grad_qkv, (((0,), (0,)),...  113 us
    unnamed x7, waiting for transfers between devices  85.6 us
    all_gather x1, waiting for transfers between devices, body(): lax.all_gather(frames, 'seq', axis=0, tiled=True)  53.4 us
    all_gather x1, waiting for transfers between devices, body(): lax.all_gather(projected[:, 2 * head_cols:], 'seq', axis=0, tiled=True)  41.4 us
    psum x1, waiting for transfers between devices, body(): w_total = lax.psum(w_part, 'dp').astype(jnp.float32)  35.2 us
    all_gather x1, blocking collectives, body(): lax.all_gather(doc_low, 'seq', axis=0, tiled=True)  18 us
    all_gather x1, blocking collectives, body(): lax.all_gather(new_docs, 'seq', axis=0, tiled=True)  16.5 us
    unnamed x19, local copies, waits for them, and re-layouts  12.6 us
  transfers between devices with their start and end apart: 6, of which 6 were waited for; matrix products, arithmetic and copies ran while one was open for 4% of the time, Pallas kernels for 0%

commit v1 on v0

v1 whole, which is shorter than its diff:
```python
import functools
import math

import jax
import jax.numpy as jnp
from jax import lax
from jax.experimental import pallas as pl
from jax.experimental.pallas import tpu as pltpu
from jax.sharding import PartitionSpec as P

HEADS = 8
HEAD = 128
BLOCK = 128
DOCS = 6
EPS = 1e-05
FACTOR = 1.0 / math.sqrt(HEAD)
MESH = pl.DeviceIdType.MESH
VMEM_LIMIT = 56 * 1024 * 1024
NT = (((1,), (1,)), ((), ()))
TN = (((0,), (0,)), ((), ()))


def remote(src, dst, send, recv, **where):
    return pltpu.make_async_remote_copy(
        src_ref=src, dst_ref=dst, send_sem=send, recv_sem=recv, device_id=where, device_id_type=MESH
    )


def gather_kernel(
    n, frames, grads, docs, all_frames, head_grads, all_docs,
    own_sem, zs, zr, ys, yr, gs, gr, ds, dr,
):
    me = lax.axis_index("seq")
    partner = me + 1 - 2 * lax.rem(me, 2)
    half = n // 2
    peers = [lax.rem(me + k, n) for k in range(1, n)]

    def head_of(device):
        start = pl.multiple_of(lax.rem(device, HEADS) * HEAD, HEAD)
        return grads.at[:, pl.ds(start, HEAD)]

    barrier = pltpu.get_barrier_semaphore()
    for peer in peers:
        pl.semaphore_signal(barrier, inc=1, device_id={"seq": peer}, device_id_type=MESH)
    own = [
        pltpu.make_async_copy(frames, all_frames.at[me], own_sem.at[0]),
        pltpu.make_async_copy(head_of(me), head_grads.at[me], own_sem.at[1]),
        pltpu.make_async_copy(docs, all_docs.at[me], own_sem.at[2]),
    ]
    for copy in own:
        copy.start()
    pl.semaphore_wait(barrier, n - 1)

    column = [
        remote(frames, all_frames.at[me], zs.at[k - 1], zr.at[k - 1], seq=lax.rem(me + 2 * k, n))
        for k in range(1, half)
    ]
    across = [remote(frames, all_frames.at[me], ys.at[0], yr.at[0], seq=partner)]
    for copy in column + across:
        copy.start()
    rest = []
    for k in range(1, n):
        rest.append(remote(docs, all_docs.at[me], ds.at[k - 1], dr.at[k - 1], seq=peers[k - 1]))
        rest.append(
            remote(head_of(peers[k - 1]), head_grads.at[me], gs.at[k - 1], gr.at[k - 1], seq=peers[k - 1])
        )
    for copy in rest:
        copy.start()
    for k in range(1, half):
        column[k - 1].wait_recv()
        block = lax.rem(me - 2 * k + n, n)
        forward = remote(all_frames.at[block], all_frames.at[block], ys.at[k], yr.at[k], seq=partner)
        forward.start()
        across.append(forward)
    for copy in own:
        copy.wait()
    for copy in column:
        copy.wait_send()
    for copy in across + rest:
        copy.wait()


def gather(n, frames, grads, docs):
    rows, width = frames.shape
    dma = pltpu.SemaphoreType.DMA
    any_spec = pl.BlockSpec(memory_space=pl.ANY)
    return pl.pallas_call(
        functools.partial(gather_kernel, n),
        out_shape=(
            jax.ShapeDtypeStruct((n, rows, width), jnp.bfloat16),
            jax.ShapeDtypeStruct((n, rows, HEAD), jnp.bfloat16),
            jax.ShapeDtypeStruct((n, 1, rows), jnp.int32),
        ),
        in_specs=[any_spec] * 3,
        out_specs=(any_spec,) * 3,
        scratch_shapes=[
            dma((3,)), dma((n // 2,)), dma((n // 2,)), dma((n // 2,)), dma((n // 2,)),
            dma((n,)), dma((n,)), dma((n,)), dma((n,)),
        ],
        compiler_params=pltpu.CompilerParams(collective_id=0, has_side_effects=True),
        name="gather",
    )(frames, grads, docs)


def normalized(frames, gain):
    values = frames.astype(jnp.float32)
    inverse = lax.rsqrt(jnp.mean(values * values, axis=-1, keepdims=True) + EPS)
    unit = values * inverse
    return inverse, unit, (unit * gain).astype(jnp.bfloat16)


def head_kernel(
    n, packing, head, frames, gain, wq, wk, wv, docs, grads, g_out, w_out,
    normed_s, q_s, k_s, v_s, g_s, pos_s, dk_s, dv_s,
):
    step = pl.program_id(0)
    rows = pl.ds(pl.multiple_of(step * BLOCK, BLOCK), BLOCK)
    normed = normalized(frames[0], gain[...])[2]
    normed_s[rows, :] = normed
    for weight, kept in ((wq, q_s), (wk, k_s), (wv, v_s)):
        kept[rows, :] = jnp.dot(normed, weight[...], preferred_element_type=jnp.float32).astype(
            jnp.bfloat16
        )
    pos_s[rows, :] = packing[step] * BLOCK + lax.broadcasted_iota(jnp.int32, (BLOCK, BLOCK), 0)

    @pl.when(step == n - 1)
    def attention():
        numbers = docs[...]
        lane = lax.broadcasted_iota(jnp.int32, (1, BLOCK), 1)
        counts = [
            jnp.sum((numbers == d).astype(jnp.float32)).astype(jnp.int32) for d in range(DOCS - 1)
        ]
        dk_s[...] = jnp.zeros_like(dk_s)
        dv_s[...] = jnp.zeros_like(dv_s)

        def first_of(block):
            own = docs[block]
            start = jnp.zeros_like(own)
            for d in range(DOCS - 1):
                start = start + jnp.where(own > d, counts[d], 0)
            return start

        def queries(i, carry):
            low, high = packing[2 * i], packing[2 * i + 1]
            first = jnp.concatenate([first_of(low), first_of(high)], axis=1)
            last = jnp.concatenate([low * BLOCK + lane, high * BLOCK + lane], axis=1)
            here = pl.ds(pl.multiple_of(i * 2 * BLOCK, 2 * BLOCK), 2 * BLOCK)
            q = q_s[here, :]
            g = grads[pl.ds(2 * i, 2)].reshape(2 * BLOCK, HEAD)
            pos = jnp.concatenate([pos_s[...], pos_s[...]], axis=1)
            scores = lax.dot_general(k_s[...], q, NT, preferred_element_type=jnp.float32)
            expon = jnp.where(
                (pos >= first) & (pos <= last),
                jnp.exp2(scores * (FACTOR * math.log2(math.e))),
                0.0,
            )
            prob = expon * (1.0 / jnp.sum(expon, axis=0, keepdims=True))
            prob_low = prob.astype(jnp.bfloat16)
            grad_prob = lax.dot_general(v_s[...], g, NT, preferred_element_type=jnp.float32)
            delta = jnp.sum(prob_low.astype(jnp.float32) * grad_prob, axis=0, keepdims=True)
            dscore = (prob * (grad_prob - delta)).astype(jnp.bfloat16)
            dk_s[...] += jnp.dot(dscore, q, preferred_element_type=jnp.float32)
            dv_s[...] += jnp.dot(prob_low, g, preferred_element_type=jnp.float32)
            dq = lax.dot_general(dscore, k_s[...], TN, preferred_element_type=jnp.float32)
            g_s[here, :HEAD] = (dq * FACTOR).astype(jnp.bfloat16)
            return carry

        lax.fori_loop(0, n // 2, queries, 0)
        g_s[:, HEAD : 2 * HEAD] = (dk_s[...] * FACTOR).astype(jnp.bfloat16)
        g_s[:, 2 * HEAD :] = dv_s[...].astype(jnp.bfloat16)
        g_out[...] = g_s[...].reshape(g_out.shape)
        w_out[...] = (
            lax.dot_general(normed_s[...], g_s[...], TN, preferred_element_type=jnp.float32)
            .astype(jnp.bfloat16)
            .reshape(w_out.shape)
        )


def head_grads_of(n, packing, head, all_frames, gain, w_qkv, all_docs, head_grads):
    width = all_frames.shape[2]
    total = n * BLOCK

    def weight(j):
        return pl.BlockSpec((width, HEAD), lambda r, packing, head: (0, j * HEADS + head[0]))

    def whole(shape):
        return pl.BlockSpec(shape, lambda r, packing, head: (0,) * len(shape))

    return pl.pallas_call(
        functools.partial(head_kernel, n),
        grid_spec=pltpu.PrefetchScalarGridSpec(
            num_scalar_prefetch=2,
            grid=(n,),
            in_specs=[
                pl.BlockSpec((1, BLOCK, width), lambda r, packing, head: (packing[r], 0, 0)),
                whole((1, width)),
                weight(0), weight(1), weight(2),
                whole((n, 1, BLOCK)),
                whole((n, BLOCK, HEAD)),
            ],
            out_specs=(whole((n, BLOCK, 3 * HEAD)), whole((n, width // n, 3 * HEAD))),
            scratch_shapes=[
                pltpu.VMEM((total, width), jnp.bfloat16),
                pltpu.VMEM((total, HEAD), jnp.bfloat16),
                pltpu.VMEM((total, HEAD), jnp.bfloat16),
                pltpu.VMEM((total, HEAD), jnp.bfloat16),
                pltpu.VMEM((total, 3 * HEAD), jnp.bfloat16),
                pltpu.VMEM((total, BLOCK), jnp.int32),
                pltpu.VMEM((total, HEAD), jnp.float32),
                pltpu.VMEM((total, HEAD), jnp.float32),
            ],
        ),
        out_shape=(
            jax.ShapeDtypeStruct((n, BLOCK, 3 * HEAD), jnp.bfloat16),
            jax.ShapeDtypeStruct((n, width // n, 3 * HEAD), jnp.bfloat16),
        ),
        compiler_params=pltpu.CompilerParams(vmem_limit_bytes=VMEM_LIMIT),
        name="head_grads",
    )(packing, head, all_frames, gain, w_qkv, w_qkv, w_qkv, all_docs, head_grads)


def halvings(rows, groups):
    sizes = []
    for _ in range(groups.bit_length() - 1):
        halved = rows % 32 == 0
        rows = rows // 2 if halved else rows
        sizes.append((rows, halved))
    return sizes


def exchange_kernel(n, groups, g_in, w_in, g_all, w_all, *scratch):
    sizes = halvings(w_in.shape[1], groups)
    count = len(sizes)
    landed, sums = scratch[:count], scratch[count : 2 * count]
    own_sem, gs, gr, ws, wr, ps, pr, bs, br = scratch[2 * count :]
    me = lax.axis_index("seq")
    dp = lax.axis_index("dp")
    peers = [lax.rem(me + k, n) for k in range(1, n)]
    bits = [lax.rem(dp // (1 << b), 2) for b in range(count)]
    partners = [dp + (1 << b) * (1 - 2 * bits[b]) for b in range(count)]

    barrier = pltpu.get_barrier_semaphore()
    for peer in peers:
        pl.semaphore_signal(barrier, inc=1, device_id={"seq": peer}, device_id_type=MESH)
    for partner in partners:
        pl.semaphore_signal(barrier, inc=1, device_id={"dp": partner}, device_id_type=MESH)
    own_g = pltpu.make_async_copy(g_in.at[me], g_all.at[me], own_sem.at[0])
    own_g.start()
    pl.semaphore_wait(barrier, n - 1 + count)

    held, offset, waits = w_in, 0, []
    for b, (size, halved) in enumerate(sizes):
        other = pl.multiple_of((1 - bits[b]) * size, size) if halved else 0
        mine = pl.multiple_of(bits[b] * size, size) if halved else 0
        send = remote(
            held.at[:, pl.ds(other, size), :], landed[b], ws.at[b], wr.at[b], dp=partners[b]
        )
        send.start()
        if b == 0:
            for k in range(1, n):
                copy = remote(
                    g_in.at[peers[k - 1]], g_all.at[me], gs.at[k - 1], gr.at[k - 1], seq=peers[k - 1]
                )
                copy.start()
                waits.append(copy)
        send.wait_recv()
        sums[b][...] = (
            held[:, pl.ds(mine, size), :].astype(jnp.float32) + landed[b][...].astype(jnp.float32)
        ).astype(jnp.bfloat16)
        send.wait_send()
        held, offset = sums[b], offset + mine
    size = sizes[-1][0]
    here = pl.ds(pl.multiple_of(offset, size), size)
    own_w = pltpu.make_async_copy(held.at[me], w_all.at[me, here, :], own_sem.at[1])
    own_w.start()
    parts = []
    for k in range(1, n):
        copy = remote(
            held.at[peers[k - 1]], w_all.at[me, here, :], ps.at[k - 1], pr.at[k - 1], seq=peers[k - 1]
        )
        copy.start()
        parts.append(copy)
    own_w.wait()
    for copy in parts:
        copy.wait()
    for b in reversed(range(count)):
        size, halved = sizes[b]
        if halved:
            here = pl.ds(pl.multiple_of(offset, size), size)
            copy = remote(
                w_all.at[:, here, :], w_all.at[:, here, :], bs.at[b], br.at[b], dp=partners[b]
            )
            copy.start()
            copy.wait()
            offset = offset - bits[b] * size
    own_g.wait()
    for copy in waits:
        copy.wait()


def exchange(n, groups, g_in, w_in):
    rows = w_in.shape[1]
    dma = pltpu.SemaphoreType.DMA
    sizes = halvings(rows, groups)
    count = len(sizes)
    any_spec = pl.BlockSpec(memory_space=pl.ANY)
    buffers = [pltpu.VMEM((n, size, 3 * HEAD), jnp.bfloat16) for size, _ in sizes]
    return pl.pallas_call(
        functools.partial(exchange_kernel, n, groups),
        out_shape=(
            jax.ShapeDtypeStruct(g_in.shape, jnp.bfloat16),
            jax.ShapeDtypeStruct(w_in.shape, jnp.bfloat16),
        ),
        in_specs=[any_spec, pl.BlockSpec(memory_space=pltpu.VMEM)],
        out_specs=(any_spec, any_spec),
        scratch_shapes=buffers + buffers + [
            dma((2,)), dma((n,)), dma((n,)), dma((count,)), dma((count,)),
            dma((n,)), dma((n,)), dma((count,)), dma((count,)),
        ],
        compiler_params=pltpu.CompilerParams(
            collective_id=1, has_side_effects=True, vmem_limit_bytes=VMEM_LIMIT
        ),
        name="exchange",
    )(g_in, w_in)


def finish_kernel(scale, packing, head, frames, gain, g_all, w_all, w_qkv, d_out, w_out, total):
    j = pl.program_id(0)
    columns = jnp.concatenate([g_all[h] for h in range(HEADS)], axis=1)
    part = lax.dot_general(columns, w_qkv[...], NT, preferred_element_type=jnp.float32)
    for h in range(HEADS):
        w_out[:, h * HEAD : (h + 1) * HEAD] = w_all[h].astype(jnp.float32) * scale

    @pl.when(j == 0)
    def first():
        total[...] = part

    @pl.when(j > 0)
    def later():
        total[...] += part

    @pl.when(j == 2)
    def last():
        inverse, unit, _ = normalized(frames[0], gain[...])
        gained = total[...] * gain[...]
        mean = jnp.mean(gained * unit, axis=-1, keepdims=True)
        d_out[...] = (inverse * (gained - unit * mean)).astype(jnp.bfloat16)


def finish(n, scale, packing, index, all_frames, gain, w_qkv, g_all, w_all):
    width = all_frames.shape[2]
    rows = w_all.shape[1]
    return pl.pallas_call(
        functools.partial(finish_kernel, scale),
        grid_spec=pltpu.PrefetchScalarGridSpec(
            num_scalar_prefetch=2,
            grid=(3,),
            in_specs=[
                pl.BlockSpec((1, BLOCK, width), lambda j, packing, index: (packing[index[0]], 0, 0)),
                pl.BlockSpec((1, width), lambda j, packing, index: (0, 0)),
                pl.BlockSpec((n, BLOCK, HEAD), lambda j, packing, index: (0, 0, j)),
                pl.BlockSpec((n, rows, HEAD), lambda j, packing, index: (0, 0, j)),
                pl.BlockSpec((width, HEADS * HEAD), lambda j, packing, index: (0, j)),
            ],
            out_specs=(
                pl.BlockSpec((BLOCK, width), lambda j, packing, index: (0, 0)),
                pl.BlockSpec((rows, HEADS * HEAD), lambda j, packing, index: (0, j)),
            ),
            scratch_shapes=[pltpu.VMEM((BLOCK, width), jnp.float32)],
        ),
        out_shape=(
            jax.ShapeDtypeStruct((BLOCK, width), jnp.bfloat16),
            jax.ShapeDtypeStruct((rows, 3 * HEADS * HEAD), jnp.float32),
        ),
        compiler_params=pltpu.CompilerParams(vmem_limit_bytes=VMEM_LIMIT),
        name="finish",
    )(packing, index, all_frames, gain, g_all, w_all, w_qkv)


def body(n, groups, layer_rows, doc_ids, packing, norm_gain, w_qkv, d_attn):
    index = lax.axis_index("seq").astype(jnp.int32).reshape(1)
    order = packing[0]
    gain = norm_gain.reshape(1, -1)
    all_frames, head_grads, all_docs = gather(n, layer_rows[0], d_attn[0], doc_ids)
    g_in, w_in = head_grads_of(
        n, order, lax.rem(index, HEADS), all_frames, gain, w_qkv, all_docs, head_grads
    )
    g_all, w_all = exchange(n, groups, g_in, w_in)
    scale = 1.0 / math.sqrt(n * BLOCK * groups)
    d_frames, w_grad = finish(n, scale, order, index, all_frames, gain, w_qkv, g_all, w_all)
    return d_frames[None], w_grad


def solution(mesh):
    return jax.shard_map(
        functools.partial(body, mesh.shape["seq"], mesh.shape["dp"]),
        mesh=mesh,
        in_specs=(
            P("dp", "seq", None),
            P("dp", "seq"),
            P("dp", None),
            P(),
            P(),
            P("dp", "seq", None),
        ),
        out_specs=(P("dp", "seq", None), P("seq", None)),
        check_vma=False,
    )
```

time: 448 us -> 101 us (0.23)
  waiting for transfers between devices: 339 us -> 0 us
  Pallas kernels: 0 us -> 100 us
  blocking collectives: 34.5 us -> 0 us
  matrix products: 27.3 us -> 0 us
  local copies, waits for them, and re-layouts: 24.6 us -> 0 us
  between operations: 14.3 us -> 0.65 us
  other arithmetic: 7.09 us -> 0 us
    reduce_scatter x1 -> x0, waiting for transfers between devices: 113 us -> none  [body(): lax.psum_scatter(rounded(lax.dot_general(normed, grad_qkv, (((0,), (0,)),...]
    all_gather x3 -> x0, waiting for transfers between devices: 105 us -> none  [the longest x1 53.4 us: body(): lax.all_gather(frames, 'seq', axis=0, tiled=True)]
    pallas_call x0 -> x4, Pallas kernels: none -> 100 us  [the longest x1 39.4 us: gather(): pl.pallas_call(functools.partial(gather_kernel, n), out_shape=(jax.ShapeD...]
    unnamed x7 -> x0, waiting for transfers between devices: 85.6 us -> none
    psum x1 -> x0, waiting for transfers between devices: 35.2 us -> none  [body(): w_total = lax.psum(w_part, 'dp').astype(jnp.float32)]
    all_gather x2 -> x0, blocking collectives: 34.5 us -> none  [the longest x1 18 us: body(): lax.all_gather(doc_low, 'seq', axis=0, tiled=True)]
    dot_general x9 -> x0, matrix products: 27.3 us -> none  [the longest x1 5.08 us: body(): lax.dot_general(grad_qkv, w_qkv, (((1,), (1,)), ((), ())), preferred_elem...]
    unnamed x19 -> x0, local copies, waits for them, and re-layouts: 12.6 us -> none
  transfers between devices with their start and end apart: 6 -> 0, of which waited for: 6 -> 0; matrix products, arithmetic and copies ran while one was open for 4% -> 0% of each run, Pallas kernels for 0% -> 0%
where the time goes in v1:
time: 101 us
  Pallas kernels  100 us (99%)
    pallas_call x1, Pallas kernels, gather(): pl.pallas_call(functools.partial(gather_kernel, n), out_shape=(jax.ShapeD...  39.4 us
    pallas_call x1, Pallas kernels, exchange(): pl.pallas_call(functools.partial(exchange_kernel, n, groups), out_shape=(...  38 us
    pallas_call x1, Pallas kernels, head_grads_of(): pl.pallas_call(functools.partial(head_kernel, n), grid_spec=pltpu.Prefetc...  15.5 us
    pallas_call x1, Pallas kernels, finish(): pl.pallas_call(functools.partial(finish_kernel, scale), grid_spec=pltpu.P...  7.47 us

profile of v1, /device:TPU:0, one launch (start us, length us, event | category | flops | bytes accessed | tf_op | source)
XLA Modules:
  0.0 101.0 jit_solution(14197118094496451954)
XLA Ops:
  0.6 39.4 %gather.1 = (bf16[8,128,1024]{2,1,0:T(8,128)(2,1)}, bf16[8,128,128]{2,1,0:T(8,128)(2,1)}, s32[8,1,128]{2,1,0:T(1,128)}) custom-call(bf16[128,1024]{1,0:T(8,128)(2,1)} %bitcast.6, bf16[128,1024]{1,0:T(8,128)(2,1)} %bitcast.7, s32[1,128]{1,0:T(1,128)} %docs.1), custom_call_target="tpu_custom_call" | custom-call | tf_op jit(solution)/shard_map/gather/pallas_call | solution.py:87
  40.1 15.5 %head_grads.1 = (bf16[8,128,384]{2,1,0:T(8,128)(2,1)}, bf16[8,128,384]{2,1,0:T(8,128)(2,1)}) custom-call(s32[8]{0:T(128)} %bitcast.10, s32[1]{0:T(128)S(6)} %rem.18.head, bf16[8,128,1024]{2,1,0:T(8,128)(2,1)} %get-tuple-element.11.frames, f32[1,1024]{1,0:T(1,128)} %bitcast.8, bf16[1024,3072]{1,0:T(8,128)(2,1)} %w_qkv.1, bf16[1024,3072]{1,0:T(8,128)(2,1)} %w_qkv.1, ...), custom_call_target="tpu_custom_call" | custom-call | tf_op jit(solution)/shard_map/head_grads/pallas_call | solution.py:189
  55.6 38.0 %exchange.1 = (bf16[8,128,384]{2,1,0:T(8,128)(2,1)}, bf16[8,128,384]{2,1,0:T(8,128)(2,1)}) custom-call(bf16[8,128,384]{2,1,0:T(8,128)(2,1)} %get-tuple-element.14.g_in, bf16[8,128,384]{2,1,0:T(8,128)(2,1)} %get-tuple-element.15.w_in), custom_call_target="tpu_custom_call" | custom-call | tf_op jit(solution)/shard_map/exchange/pallas_call | solution.py:308
  93.5 7.5 %finish.1 = (bf16[128,1024]{1,0:T(8,128)(2,1)}, f32[128,3072]{1,0:T(8,128)}) custom-call(s32[8]{0:T(128)} %bitcast.11, s32[1]{0:T(128)} %bitcast.1.head, bf16[8,128,1024]{2,1,0:T(8,128)(2,1)} %get-tuple-element.11.frames, f32[1,1024]{1,0:T(1,128)} %bitcast.9, bf16[8,128,384]{2,1,0:T(8,128)(2,1)} %get-tuple-element.16.g_all, ...), custom_call_target="tpu_custom_call" | custom-call | tf_op jit(solution)/shard_map/finish/pallas_call | solution.py:353
